TPU v7x, 256 devices: a whole 4x4x8 slice. The times are simulated.
256 devices in a mesh: grp: 4 (over x_lo, core), blk: 4 (over y), head: 16 (over z, x_hi).
Axes of the slice: x: 4 (x_hi: 2, x_lo: 2; x = x_hi * 2 + x_lo), y: 4, z: 8, core: 2. Of those that a mesh axis runs over, the one named last changes fastest.
Arguments:
- enc_states: bfloat16 [512, 4096], P(('grp', 'blk', 'head')), may hold values from -6 to 6
- image_count: int32 [4], P('grp'), may hold values from 1 to 64
- prompt_count: int32 [4], P('grp'), may hold values from 1 to 64
- enc_gain: float32 [4096], replicated, may hold values from 0.5 to 2
- enc_gate: bfloat16 [4096, 14336], P(None, ('blk', 'head')), may hold values from -0.09375 to 0.09375
- enc_up: bfloat16 [4096, 14336], P(None, ('blk', 'head')), may hold values from -0.09375 to 0.09375
- enc_down: bfloat16 [14336, 4096], P(('blk', 'head')), may hold values from -0.046875 to 0.046875
- final_gain: float32 [4096], P(('blk', 'head')), may hold values from 0.5 to 2
- w_in: bfloat16 [4096, 3072], P(('blk', 'head')), may hold values from -0.09375 to 0.09375
- mod_text: float32 [4, 2, 3072], P('grp'), may hold values from -2.5 to 2.5
- mod_video: float32 [4, 2, 3072], P('grp'), may hold values from -2.5 to 2.5
- w_kv_text: bfloat16 [3072, 16, 256], P(None, 'head'), may hold values from -0.109375 to 0.109375
- w_qkv: bfloat16 [3072, 16, 384], P(None, 'head'), may hold values from -0.07252963 to 0.07252963
- query_gain: float32 [128], replicated, may hold values from 0.5 to 6
- key_gain: float32 [128], replicated, may hold values from 0.5 to 6
- text_key_gain: float32 [128], replicated, may hold values from 0.5 to 3
- video_states: bfloat16 [32768, 3072], P(('grp', 'blk', 'head')), may hold values from -6 to 6
Outputs:
- attended: bfloat16 [32768, 2048], P(('grp', 'blk', 'head'))
All inputs are finite; a program needn't handle non-finite values.
Results may differ from a plain program's by a relative error of at most 0.005.
The roundings to bfloat16 on the way count: a program that leaves them out, or rounds other values in their place, can miss the bound.
Values may be sent and summed in bfloat16 or wider, within the bound.
A program may use at most 192 MiB of HBM per device.

v0:
```python
import jax
import jax.numpy as jnp
from jax import lax
from jax.sharding import PartitionSpec as P

IMG_ROWS = 64


epsilon = 1e-06
negative = -1e30


def from_behind(block, axis, distance):
    devices = range(lax.axis_size(axis))
    route = [((i - distance) % len(devices), i) for i in devices]
    return lax.ppermute(block, axis, route)


def rms_norm(values, scale):
    return values * lax.rsqrt(jnp.mean(values * values, axis=-1, keepdims=True) + epsilon) * scale


def layer_norm(values):
    center = values - jnp.mean(values, axis=-1, keepdims=True)
    return center * lax.rsqrt(jnp.mean(center * center, axis=-1, keepdims=True) + epsilon)


def attend_block(carry, queries, keys, values, allowed, head_dim):
    running, total, output = carry
    scores = jnp.einsum(
        "qhe,khe->hqk", queries, keys, preferred_element_type=jnp.float32
    ) * head_dim ** (-0.5)
    scores = jnp.where(allowed[None, None, :], scores, negative)
    highest = jnp.maximum(running, jnp.max(scores, axis=-1))
    factor = jnp.exp(running - highest)
    weights = jnp.exp(scores - highest[..., None])
    total = total * factor + jnp.sum(weights, axis=-1)
    output = output * factor[..., None] + jnp.einsum(
        "hqk,khe->hqe", weights.astype(jnp.bfloat16), values, preferred_element_type=jnp.float32
    )
    return (highest, total, output)


def local(
    enc_states,
    image_count,
    prompt_count,
    enc_gain,
    enc_gate,
    enc_up,
    enc_down,
    final_gain,
    w_in,
    mod_text,
    mod_video,
    w_kv_text,
    w_qkv,
    query_gain,
    key_gain,
    text_key_gain,
    video_states,
):
    enc_float = enc_states.astype(jnp.float32)
    normed = rms_norm(enc_float, enc_gain).astype(jnp.bfloat16)
    piece = lax.all_gather(normed, ("blk", "head"), axis=0, tiled=True)
    gate = jnp.dot(piece, enc_gate, preferred_element_type=jnp.float32)
    upward = jnp.dot(piece, enc_up, preferred_element_type=jnp.float32)
    hidden = (jax.nn.silu(gate) * upward).astype(jnp.bfloat16)
    local_rows = enc_states.shape[0]
    offset = lax.axis_index(("blk", "head")) * local_rows
    term = jnp.dot(hidden, enc_down, preferred_element_type=jnp.float32)
    own_part = lax.dynamic_slice_in_dim(term, offset, local_rows, 0) + enc_float
    term = lax.dynamic_update_slice_in_dim(term, own_part, offset, 0)
    enc_out = lax.psum_scatter(term, ("blk", "head"), scatter_dimension=1, tiled=True)
    squares = jnp.sum(enc_out * enc_out, axis=-1)
    scaled = (enc_out * final_gain).astype(jnp.bfloat16)
    partial_rows = jnp.dot(scaled, w_in, preferred_element_type=jnp.float32)
    full_width = enc_states.shape[1]
    head_dim = query_gain.shape[0]
    total_squares, refined = lax.psum((squares, partial_rows), ("blk", "head"))
    condition = refined * lax.rsqrt(total_squares / full_width + epsilon)[:, None]
    cond_mod = (layer_norm(condition) * (1.0 + mod_text[0, 1]) + mod_text[0, 0]).astype(
        jnp.bfloat16
    )
    text_kv = jnp.einsum("ld,dhe->lhe", cond_mod, w_kv_text, preferred_element_type=jnp.float32)
    text_normed = rms_norm(text_kv[..., :head_dim], text_key_gain)
    text_both = jnp.concatenate([text_normed, text_kv[..., head_dim:]], axis=-1).astype(
        jnp.bfloat16
    )
    text_keys = text_both[..., :head_dim]
    text_values = text_both[..., head_dim:]
    cond_rows = jnp.arange(text_both.shape[0], dtype=jnp.int32)
    live = jnp.where(
        cond_rows < IMG_ROWS, cond_rows < image_count[0], cond_rows - IMG_ROWS < prompt_count[0]
    )
    video_mod = (
        layer_norm(video_states.astype(jnp.float32)) * (1.0 + mod_video[0, 1]) + mod_video[0, 0]
    ).astype(jnp.bfloat16)
    mixed = jnp.einsum(
        "td,dhe->the",
        lax.all_gather(video_mod, "head", axis=0, tiled=True),
        w_qkv,
        preferred_element_type=jnp.float32,
    )
    queries = rms_norm(mixed[..., :head_dim], query_gain)
    keys = rms_norm(mixed[..., head_dim : 2 * head_dim], key_gain)
    projected = jnp.concatenate([queries, keys, mixed[..., 2 * head_dim :]], axis=-1).astype(
        jnp.bfloat16
    )
    queries = projected[..., :head_dim]
    keys = projected[..., head_dim : 2 * head_dim]
    values = projected[..., 2 * head_dim :]
    block_rows = projected.shape[0]
    local_heads = projected.shape[1]
    initial = (
        jnp.full((local_heads, block_rows), negative, jnp.float32),
        jnp.zeros((local_heads, block_rows), jnp.float32),
        jnp.zeros((local_heads, block_rows, head_dim), jnp.float32),
    )
    every_key = jnp.ones((block_rows,), dtype=bool)
    carry = initial
    carry = attend_block(carry, queries, keys, values, every_key, head_dim)
    passing = jnp.concatenate([keys, values], axis=-1)
    for turn in range(lax.axis_size("blk") - 1):
        passing = from_behind(passing, "blk", 1)
        carry = attend_block(
            carry, queries, passing[..., :head_dim], passing[..., head_dim:], every_key, head_dim
        )
    carry = attend_block(carry, queries, text_keys, text_values, live, head_dim)
    output = carry[2] / carry[1][..., None]
    output = (
        jnp.transpose(output, (1, 0, 2))
        .reshape(block_rows, local_heads * head_dim)
        .astype(jnp.bfloat16)
    )
    return lax.all_to_all(output, "head", split_axis=0, concat_axis=1, tiled=True)


def solution(mesh):
    placed = (
        P(("grp", "blk", "head"), None),
        P("grp"),
        P("grp"),
        P(),
        P(None, ("blk", "head")),
        P(None, ("blk", "head")),
        P(("blk", "head"), None),
        P(("blk", "head")),
        P(("blk", "head"), None),
        P("grp", None, None),
        P("grp", None, None),
        P(None, "head", None),
        P(None, "head", None),
        P(),
        P(),
        P(),
        P(("grp", "blk", "head"), None),
    )
    return jax.shard_map(
        local,
        mesh=mesh,
        in_specs=placed,
        out_specs=P(("grp", "blk", "head"), None),
        check_vma=False,
    )
```

profile of v0, /device:TPU:24, one launch (start us, length us, event | category | flops | bytes accessed | tf_op | source)
XLA Modules:
  0.0 1604.3 jit_solution(2949825063173910119)
XLA Ops:
  7.4 1.0 fusion.87
  8.4 1.4 fusion.99
  9.9 118.7 %all-gather.6.cloned.1.call-done = bf16[64,2,4096]{2,1,0:T(2,128)(2,1)} async-done(((bf16[1,2,4096]{2,1,0:T(2,128)(2,1)}), bf16[64,2,4096]{2,1,0:T(2,128)(2,1)}) %all-gather.6.cloned.1.call-update) | async-done | bytes 1048592 | tf_op jit(solution)/shard_map/all_gather | solution.py:65
  128.6 1.5 reshape.516
  130.1 2.1 fusion.110
  132.2 5.0 fusion.63
  137.2 1.6 fusion.90
  138.9 2.9 copy.20
  141.9 1.3 convert_reduce_fusion
  143.2 1.5 fusion.53
  144.7 0.8 slice_add_fusion.1
  145.5 1.3 fusion.56
  148.2 0.5 compare_select_fusion
  148.7 1.4 slice_add_fusion
  150.1 415.6 %reduce-scatter.4.cloned.1.call-done = f32[64,128]{1,0:T(8,128)} async-done(((f32[4096,128]{1,0:T(8,128)}), f32[64,128]{1,0:T(8,128)}) %reduce-scatter.4.cloned.1.call-update) | async-done | bytes 32784
  565.8 0.8 copy.21
  566.7 178.5 %psum.15 = f32[128]{0:T(128)S(1)} all-reduce(f32[128]{0:T(128)S(1)} %multiply_reduce_fusion.9), channel_id=1, replica_groups=mesh['grp'=4,'blk'=4,'head'=16] {'blk','head'}, use_global_device_ids=true, to_apply=%region_12.13 | all-reduce | flops 128 | bytes 1024 | tf_op jit(solution)/shard_map/psum | solution.py:80
  745.3 2.1 fusion.91
  747.5 8.1 convolution_bitcast_fusion
  755.7 0.2 multiply_reduce_fusion.6
  755.9 1.4 copy-done.2
  757.3 0.2 multiply_convert_fusion
  757.5 1.1 pad_maximum_fusion
  758.6 30.8 %collective-permute-start = (bf16[2048,1,256]{0,2,1:T(8,128)(2,1)}, bf16[2048,1,256]{0,2,1:T(8,128)(2,1)S(1)}, u32[]{:S(2)}, u32[]{:S(2)}) collective-permute-start(bf16[2048,1,256]{0,2,1:T(8,128)(2,1)} %pad_maximum_fusion), channel_id=1, source_target_pairs={{48,0},{0,16},{16,32},{32,48},{49,1},{1,17},{17,33},{33,49},{50,2}... | collective-permute-start | bytes 3145736 | tf_op jit(solution)/shard_map/ppermute | solution.py:16
  789.4 658.3 %all-reduce.2.cloned.1.call-done = f32[128,3072]{1,0:T(8,128)} async-done(((f32[128,3072]{1,0:T(8,128)}), f32[128,3072]{1,0:T(8,128)}) %all-reduce.2.cloned.1.call-update) | async-done | bytes 1572880 | tf_op jit(solution)/shard_map/psum | solution.py:80
  1447.8 1.7 multiply_reduce_fusion.5
  1449.4 1.8 multiply_reduce_fusion.4
  1451.2 2.4 fusion.59
  1453.7 22.1 %collective-permute-start.1 = (bf16[2048,1,256]{0,2,1:T(8,128)(2,1)S(1)}, bf16[2048,1,256]{0,2,1:T(8,128)(2,1)S(1)}, u32[]{:S(2)}, u32[]{:S(2)}) collective-permute-start(bf16[2048,1,256]{0,2,1:T(8,128)(2,1)S(1)} %collective-permute-done), channel_id=1, source_target_pairs={{48,0},{0,16},{16,32},{32,48},{49,1},{1,17},{17,33},{33,49},{50,2}... | collective-permute-start | bytes 3145736 | tf_op jit(solution)/shard_map/ppermute | solution.py:16
  1475.9 0.4 fusion.108
  1476.2 8.1 multiply_reduce_fusion.3
  1484.3 3.9 collective-permute-done.1
  1488.2 3.7 collective-permute-start.2
  1491.9 8.1 multiply_reduce_fusion.2
  1499.9 8.1 multiply_reduce_fusion.1
  1508.0 8.1 multiply_reduce_fusion
  1516.1 0.3 fusion.71
  1516.6 8.5 fusion.6
  1525.2 8.8 fusion.4
  1533.9 8.6 fusion.2
  1542.5 8.6 fusion
  1551.1 8.3 fusion.20
  1559.5 7.6 fusion.26
  1567.1 0.6 slice-done.3
  1567.6 3.2 fusion.32
  1570.9 7.8 fusion.48
  1578.8 17.1 %all_to_all.16 = bf16[16,128,128]{2,1,0:T(8,128)(2,1)S(1)} all-to-all(bf16[16,128,128]{2,1,0:T(8,128)(2,1)S(1)} %bitcast.88), channel_id=1, replica_groups=mesh['grp'=4,'blk'=4,'head'=16] {'head'}, dimensions={0} | all-to-all | bytes 1048576 | tf_op jit(solution)/shard_map/all_to_all | solution.py:136
  1595.9 0.9 copy_bitcast_fusion
  (54 shorter events, 0.8 us)
Async XLA Ops:
  7.4 740.1 %copy-start = (bf16[3072,1,384]{2,0,1:T(8,128)(2,1)S(1)}, bf16[3072,1,384]{2,0,1:T(8,128)(2,1)}, u32[]{:S(2)}) copy-start(bf16[3072,1,384]{2,0,1:T(8,128)(2,1)} %param.29) | copy-start | bytes 7077892
  7.4 129.8 %copy-start.5 = (bf16[2,4096]{1,0:T(2,128)(2,1)S(1)}, bf16[2,4096]{1,0:T(2,128)(2,1)}, u32[]{:S(2)}) copy-start(bf16[2,4096]{1,0:T(2,128)(2,1)} %param.17) | copy-start | bytes 49156
  7.4 121.2 %all-gather.6.cloned.1.call-start = ((), (), s32[]{:S(2)}) async-start(), calls=%async_computation.4 | async-start | bytes 1064960 | tf_op jit(solution)/shard_map/all_gather | solution.py:65
  9.9 555.9 %reduce-scatter.4.cloned.1.call-start = ((), (), s32[]{:S(2)}) async-start(), calls=%async_computation.5 | async-start | bytes 2129920
  137.2 8.3 copy-start.3
  137.2 608.1 %copy-start.4 = (bf16[64,3072]{1,0:T(8,128)(2,1)S(1)}, bf16[64,3072]{1,0:T(8,128)(2,1)}, u32[]{:S(2)}) copy-start(bf16[64,3072]{1,0:T(8,128)(2,1)} %param.25) | copy-start | bytes 1179652
  141.8 605.7 %all-gather.4.cloned.1.call-start = ((), (), s32[]{:S(2)}) async-start(), calls=%async_computation.2 | async-start | bytes 13369344 | tf_op jit(solution)/shard_map/all_gather | solution.py:101
  146.9 1300.9 %all-reduce.2.cloned.1.call-start = ((), (), s32[]{:S(2)}) async-start(), calls=%async_computation.3 | async-start | bytes 3145728 | tf_op jit(solution)/shard_map/psum | solution.py:80
  747.4 9.8 copy-start.7
  747.5 9.8 copy-start.8
  755.6 1.7 copy-start.2
  755.6 695.6 %copy-start.6 = (f32[1,1,3072]{2,1,0:T(1,128)S(1)}, f32[1,1,3072]{2,1,0:T(1,128)}, u32[]{:S(2)}) copy-start(f32[1,1,3072]{2,1,0:T(1,128)} %get-tuple-element.19) | copy-start | bytes 36868
  755.6 720.2 %copy-start.9 = (f32[128]{0:T(128)S(1)}, f32[128]{0:T(128)}, u32[]{:S(2)}) copy-start(f32[128]{0:T(128)} %param.32) | copy-start | bytes 1540
  755.6 720.2 %copy-start.10 = (pred[128]{0:T(512)(128)(4,1)S(1)}, pred[128]{0:T(512)(128)(4,1)}, u32[]{:S(2)}) copy-start(pred[128]{0:T(512)(128)(4,1)} %compare_select_fusion) | copy-start | bytes 388
  758.6 695.1 %collective-permute-start = (bf16[2048,1,256]{0,2,1:T(8,128)(2,1)}, bf16[2048,1,256]{0,2,1:T(8,128)(2,1)S(1)}, u32[]{:S(2)}, u32[]{:S(2)}) collective-permute-start(bf16[2048,1,256]{0,2,1:T(8,128)(2,1)} %pad_maximum_fusion), channel_id=1, source_target_pairs={{48,0},{0,16},{16,32},{32,48},{49,1},{1,17},{17,33},{33,49},{50,2}... | collective-permute-start | bytes 3145736 | tf_op jit(solution)/shard_map/ppermute | solution.py:16
  1453.7 34.5 %collective-permute-start.1 = (bf16[2048,1,256]{0,2,1:T(8,128)(2,1)S(1)}, bf16[2048,1,256]{0,2,1:T(8,128)(2,1)S(1)}, u32[]{:S(2)}, u32[]{:S(2)}) collective-permute-start(bf16[2048,1,256]{0,2,1:T(8,128)(2,1)S(1)} %collective-permute-done), channel_id=1, source_target_pairs={{48,0},{0,16},{16,32},{32,48},{49,1},{1,17},{17,33},{33,49},{50,2}... | collective-permute-start | bytes 3145736 | tf_op jit(solution)/shard_map/ppermute | solution.py:16
  1488.2 19.9 %collective-permute-start.2 = (bf16[2048,1,256]{0,2,1:T(8,128)(2,1)S(1)}, bf16[2048,1,256]{0,2,1:T(8,128)(2,1)S(1)}, u32[]{:S(2)}, u32[]{:S(2)}) collective-permute-start(bf16[2048,1,256]{0,2,1:T(8,128)(2,1)S(1)} %collective-permute-done.1), channel_id=1, source_target_pairs={{48,0},{0,16},{16,32},{32,48},{49,1},{1,17},{17,33},{33,49},{50,2}... | collective-permute-start | bytes 3145736 | tf_op jit(solution)/shard_map/ppermute | solution.py:16
  1551.1 15.9 slice-start
  1551.1 15.9 slice-start.1
  1559.4 7.6 slice-start.2
  1559.5 8.2 slice-start.3
  1570.9 25.9 %copy-start.1 = (bf16[3072,1,384]{2,0,1:T(8,128)(2,1)S(1)}, bf16[3072,1,384]{2,0,1:T(8,128)(2,1)}, u32[]{:S(2)}) copy-start(bf16[3072,1,384]{2,0,1:T(8,128)(2,1)} %param.29) | copy-start | bytes 7077892
Sparse Core Ops, SparseCore 0:
  11.7 116.8 all-gather.5
  141.9 423.7 reduce-scatter.3
  747.6 700.1 all-reduce.1
Sparse Core Ops, SparseCore 1:
  146.9 177.5 all-gather.3
where the time goes:
time: 1610 us; the launch traced here: 1600 us
  waiting for transfers between devices  1200 us (75%)
  blocking collectives  196 us (12%)
  matrix products  79.7 us (5%)
  starting transfers between devices  56.8 us (4%)
  other arithmetic  50.8 us (3%)
  between operations  16.6 us (1%)
    psum x1, waiting for transfers between devices, local(): total_squares, refined = lax.psum((squares, partial_rows), ('blk', 'head'))  658 us
    unnamed x5, waiting for transfers between devices  416 us
    psum x1, blocking collectives, local(): total_squares, refined = lax.psum((squares, partial_rows), ('blk', 'head'))  179 us
    all_gather x1, waiting for transfers between devices, local(): piece = lax.all_gather(normed, ('blk', 'head'), axis=0, tiled=True)  119 us
    ppermute x3, starting transfers between devices, from_behind(): return lax.ppermute(block, axis, route)  56.6 us
    reduce_sum x5, other arithmetic, attend_block(): total = total * factor + jnp.sum(weights, axis=-1)  34.6 us
    dot_general x5, matrix products, attend_block(): jnp.einsum('qhe,khe->hqk', queries, keys, preferred_element_type=jnp.floa...  32.7 us
  transfers between devices with their start and end apart: 7, of which 4 were waited for; matrix products, arithmetic and copies ran while one was open for 3% of the time, Pallas kernels for 0%

commit v1 on v0

v1 whole, which is shorter than its diff:
```python
import functools

import jax
import jax.numpy as jnp
from jax import lax
from jax.experimental import pallas as pl
from jax.experimental.pallas import tpu as pltpu
from jax.sharding import PartitionSpec as P

MESH = pl.DeviceIdType.MESH
EPS = 1e-06
NEG = -1e30
IMG_ROWS = 64
F32 = jnp.float32
BF16 = jnp.bfloat16
HD = 128
D = 3072
ED = 4096
STEP_CHUNKS = ((0, 1), (1, 2), (3, 2), (5, 2), (7, 1))
N_COPIES = 96


def dot(a, b):
    return jnp.dot(a, b, preferred_element_type=F32)


def dot_t(a, b):
    return lax.dot_general(a, b, (((1,), (1,)), ((), ())), preferred_element_type=F32)


def rms(values, gain):
    return values * lax.rsqrt(jnp.mean(values * values, axis=-1, keepdims=True) + EPS) * gain


class Links:
    def __init__(self, send, recv):
        self.send, self.recv, self.count, self.started = send, recv, 0, []

    def start(self, src, dst, device):
        copy = pltpu.make_async_remote_copy(
            src_ref=src,
            dst_ref=dst,
            send_sem=self.send.at[self.count],
            recv_sem=self.recv.at[self.count],
            device_id=device,
            device_id_type=MESH,
        )
        copy.start()
        self.count += 1
        self.started.append(copy)
        return copy

    def drain(self):
        for copy in self.started:
            copy.wait_send()


def front_kernel(
    enc_own, video, mod_video, mod_text, enc_gain, final_gain, query_gain, key_gain, text_gain,
    w_qkv, gate_t, up_t, down, w_in, w_kv,
    q_out, kv_out, text_out,
    tok0, tok1, tok2, tok3, tok4, w_two, g_v, u_v, d_v, wi_v, wk_v,
    xq, xkv, granules, rows_v, normed_v, term, r_term, part, r_part, part_x, r_x,
    proj, r_proj, proj_z, r_projz, proj_x, r_projx, cond,
    send, recv, local_sem,
):
    g, y, h = lax.axis_index("grp"), lax.axis_index("blk"), lax.axis_index("head")
    z, X = h // 2, h % 2
    core = g % 2
    z_at = lambda dz: (g, y, ((z + dz) % 8) * 2 + X)
    y_at = lambda dy: (g, (y + dy) % 4, h)
    x_at = (g, y, z * 2 + (1 - X))
    w_at = ((g + 2) % 4, y, z * 2 + (1 - X))
    core_at = (g + 1 - 2 * core, y, h)
    peers = [z_at(i) for i in range(1, 8)] + [y_at(i) for i in range(1, 4)] + [x_at, w_at, core_at]

    loads = [
        pltpu.make_async_copy(src, dst, local_sem.at[i])
        for i, (src, dst) in enumerate(
            [(w_qkv, w_two.at[0]), (gate_t, g_v), (up_t, u_v), (down, d_v), (w_in, wi_v), (w_kv, wk_v)]
        )
    ]
    for load in loads:
        load.start()

    barrier = pltpu.get_barrier_semaphore()
    for peer in peers:
        pl.semaphore_signal(barrier, inc=1, device_id=peer, device_id_type=MESH)
    pl.semaphore_wait(barrier, len(peers))

    links = Links(send, recv)

    granules[y, X, z] = enc_own[...]
    enc_z = [
        links.start(granules.at[y, X, z], granules.at[y, X, z], z_at(i)) for i in range(1, 8)
    ]

    scale, shift = 1.0 + mod_video[1:2, :], mod_video[0:1, :]

    def modulate(i, _):
        at = pl.ds(pl.multiple_of(i * 16, 16), 16)
        v = video[at, :].astype(F32)
        c = v - jnp.mean(v, axis=-1, keepdims=True)
        n = c * lax.rsqrt(jnp.mean(c * c, axis=-1, keepdims=True) + EPS)
        tok0[at, :] = (n * scale + shift).astype(BF16)
        return 0

    lax.fori_loop(0, 8, modulate, 0)
    toks = [tok0, tok1, tok2, tok3, tok4]

    def ring(step):
        if step == 1:
            up, down_ = tok0, tok0
        else:
            up, down_ = toks[step - 1].at[0:128], toks[step - 1].at[128:256]
        if step < 4:
            return [
                links.start(up, toks[step].at[0:128], z_at(1)),
                links.start(down_, toks[step].at[128:256], z_at(7)),
            ]
        return [
            links.start(toks[3].at[0:64], tok4.at[0:64], z_at(1)),
            links.start(toks[3].at[192:256], tok4.at[64:128], z_at(7)),
        ]

    arrivals = [None, ring(1)]
    half = pl.ds(pl.multiple_of(core * (D // 2), D // 2), D // 2)
    w_half = links.start(w_qkv.at[half], w_two.at[1, half], w_at)

    q_gain, k_gain = query_gain[...], key_gain[...]

    def project(step, which):
        first, count = STEP_CHUNKS[step]
        mixed = dot(toks[step][...], w_two[which])
        q = rms(mixed[:, :HD], q_gain).astype(BF16)
        k = rms(mixed[:, HD : 2 * HD], k_gain).astype(BF16)
        v = mixed[:, 2 * HD :].astype(BF16)
        for i in range(count):
            at = slice(i * 128, (i + 1) * 128)
            if which == 0:
                q_out[0, first + i] = q[at]
                kv_out[0, 0, first + i, 0] = k[at]
                kv_out[0, 0, first + i, 1] = v[at]
            else:
                xq[first + i] = q[at]
                xkv[first + i, 0] = k[at]
                xkv[first + i, 1] = v[at]

    y_copies, x_copies = [], {}

    def spread(step, x_rel):
        first, count = STEP_CHUNKS[step]
        for dy in (1, 3, 2):
            y_copies.append(
                links.start(
                    kv_out.at[0, x_rel, pl.ds(first, count)],
                    kv_out.at[4 - dy, x_rel, pl.ds(first, count)],
                    y_at(dy),
                )
            )

    def own_head(step):
        project(step, 0)
        spread(step, 0)

    def other_head(step):
        first, count = STEP_CHUNKS[step]
        project(step, 1)
        x_copies[step] = [
            links.start(xq.at[pl.ds(first, count)], q_out.at[1, pl.ds(first, count)], x_at),
            links.start(
                xkv.at[pl.ds(first, count)], kv_out.at[0, 1, pl.ds(first, count)], x_at
            ),
        ]

    def pass_on(step):
        for copy in x_copies[step]:
            copy.wait_recv()
        spread(step, 1)

    def arrive(step):
        for copy in arrivals[step]:
            copy.wait_recv()
        if step < 4:
            arrivals.append(ring(step + 1))

    for copy in enc_z:
        copy.wait_recv()
    enc_x = links.start(granules.at[y, X], granules.at[y, X], x_at)
    loads[0].wait()
    own_head(0)
    enc_x.wait_recv()
    enc_y = [links.start(granules.at[y], granules.at[y], y_at(i)) for i in (1, 3, 2)]

    for copy in enc_y:
        copy.wait_recv()
    out_at = lax.broadcasted_iota(jnp.int32, (256, 256), 0)
    in_at = lax.broadcasted_iota(jnp.int32, (256, 256), 1)
    order = (in_at == (out_at % 32) * 8 + out_at // 32).astype(F32).astype(BF16)
    for b in range(4):
        sorted_rows = dot(order, granules[b].reshape(256, 512)).astype(BF16)
        for j in range(8):
            rows_v[32 * b : 32 * b + 32, 512 * j : 512 * j + 512] = sorted_rows[32 * j : 32 * j + 32]

    def normalize(i, _):
        at = pl.ds(pl.multiple_of(i * 16, 16), 16)
        v = rows_v[at, :].astype(F32)
        normed_v[at, :] = rms(v, enc_gain[...]).astype(BF16)
        return 0

    lax.fori_loop(0, 8, normalize, 0)
    loads[1].wait()
    loads[2].wait()
    gate = dot_t(normed_v[...], g_v[...])
    upward = dot_t(normed_v[...], u_v[...])
    hidden = (gate / (1.0 + jnp.exp(-gate)) * upward).astype(BF16)
    loads[3].wait()
    for b in range(4):
        term[b] = dot(hidden, d_v[:, 1024 * b : 1024 * b + 1024]).astype(BF16)
    enc_ry = [links.start(term.at[(y + i) % 4], r_term.at[i - 1], y_at(i)) for i in (1, 3, 2)]

    arrive(1)
    own_head(1)

    for copy in enc_ry:
        copy.wait_recv()
    total = term[y].astype(F32)
    for i in range(3):
        total = total + r_term[i].astype(F32)
    for i in range(8):
        part[i] = total[:, 128 * i : 128 * i + 128].astype(BF16)
    enc_rz = [links.start(part.at[(z + i) % 8], r_part.at[i - 1], z_at(i)) for i in range(1, 8)]

    w_half.wait_recv()
    w_core = links.start(w_two.at[1, half], w_two.at[1, half], core_at)

    for copy in enc_rz:
        copy.wait_recv()
    total = part[z].astype(F32)
    for i in range(7):
        total = total + r_part[i].astype(F32)
    part_x[...] = total
    enc_rx = links.start(part_x, r_x, x_at)

    w_core.wait_recv()
    other_head(0)
    other_head(1)

    enc_rx.wait_recv()
    column = pl.multiple_of(y * 1024 + z * 128, 128)
    enc_out = total + r_x[...] + rows_v[:, pl.ds(column, 128)].astype(F32)
    own = jnp.where(X == 0, enc_out[:, :64], enc_out[:, 64:])
    squares = jnp.sum(own * own, axis=-1, keepdims=True)
    scaled = (own * final_gain[...]).astype(BF16)
    loads[4].wait()
    wide = jnp.broadcast_to(squares, (128, 128)).astype(BF16)
    for b in range(4):
        proj[b, :, D:] = wide[32 * b : 32 * b + 32]
    for i in range(6):
        product = dot(scaled, wi_v[:, 512 * i : 512 * i + 512]).astype(BF16)
        for b in range(4):
            proj[b, :, 512 * i : 512 * i + 512] = product[32 * b : 32 * b + 32]
    ref_y = [links.start(proj.at[(y + i) % 4], r_proj.at[i - 1], y_at(i)) for i in (1, 3, 2)]

    arrive(2)
    own_head(2)
    pass_on(0)
    pass_on(1)

    for copy in ref_y:
        copy.wait_recv()
    total = proj[y].astype(F32)
    for i in range(3):
        total = total + r_proj[i].astype(F32)
    for i in range(8):
        proj_z[i, :, :384] = total[:, 384 * i : 384 * i + 384].astype(BF16)
        proj_z[i, :, 384:] = total[:, D:].astype(BF16)
    ref_z = [links.start(proj_z.at[(z + i) % 8], r_projz.at[i - 1], z_at(i)) for i in range(1, 8)]

    other_head(2)

    for copy in ref_z:
        copy.wait_recv()
    total = proj_z[z].astype(F32)
    for i in range(7):
        total = total + r_projz[i].astype(F32)
    proj_x[...] = total
    ref_x = links.start(proj_x, r_projx, x_at)

    arrive(3)
    own_head(3)
    pass_on(2)

    ref_x.wait_recv()
    total = total + r_projx[...]
    cond[z] = (total[:, :384] * lax.rsqrt(total[:, 384:385] / ED + EPS)).astype(BF16)
    ref_all = [links.start(cond.at[z], cond.at[z], z_at(i)) for i in range(1, 8)]

    other_head(3)

    for copy in ref_all:
        copy.wait_recv()
    total = jnp.zeros((32, 1), F32)
    for i in range(8):
        total = total + jnp.sum(cond[i].astype(F32), axis=-1, keepdims=True)
    mean = total / D
    total = jnp.zeros((32, 1), F32)
    for i in range(8):
        c = cond[i].astype(F32) - mean
        total = total + jnp.sum(c * c, axis=-1, keepdims=True)
    inverse = lax.rsqrt(total / D + EPS)
    loads[5].wait()
    text = jnp.zeros((32, 256), F32)
    for i in range(8):
        at = slice(384 * i, 384 * i + 384)
        c = (cond[i].astype(F32) - mean) * inverse
        c = (c * (1.0 + mod_text[1:2, at]) + mod_text[0:1, at]).astype(BF16)
        text = text + dot(c, wk_v[at, :])
    text_out[y, 0] = rms(text[:, :HD], text_gain[...]).astype(BF16)
    text_out[y, 1] = text[:, HD:].astype(BF16)
    text_y = [links.start(text_out.at[y], text_out.at[y], y_at(i)) for i in (1, 3, 2)]

    arrive(4)
    other_head(4)
    own_head(4)
    pass_on(3)
    pass_on(4)

    for copy in text_y + y_copies:
        copy.wait_recv()
    links.drain()


def attend_kernel(q_ref, kv_ref, text_ref, bias_ref, out_ref, staged, send, recv, local_sem):
    g, y, h = lax.axis_index("grp"), lax.axis_index("blk"), lax.axis_index("head")
    z, X = h // 2, h % 2

    def peer(k):
        c, x_rel = k % 8, k // 8
        offset = (c % 2) * (8 - (c + 1) // 2) + (1 - c % 2) * (c // 2)
        return (g, y, ((z + offset) % 8) * 2 + (X + x_rel) % 2)

    barrier = pltpu.get_barrier_semaphore()
    for k in range(1, 16):
        pl.semaphore_signal(barrier, inc=1, device_id=peer(k), device_id_type=MESH)
    pl.semaphore_wait(barrier, 15)

    columns = pl.ds(pl.multiple_of(h * 128, 128), 128)

    def deliver(k):
        return pltpu.make_async_remote_copy(
            src_ref=staged.at[k],
            dst_ref=out_ref.at[:, columns],
            send_sem=send.at[k],
            recv_sem=recv.at[k],
            device_id=peer(k),
            device_id_type=MESH,
        )

    factor = HD ** (-0.5) * 1.4426950408889634
    ones = jnp.ones((1024, 128), BF16)

    def tile(i, _):
        t = 7 - i
        x_rel, c = t // 4, (t % 4) * 2
        q = q_ref[x_rel, pl.ds(c, 2)].reshape(256, 128)

        def scores_of(n):
            if n == 8:
                keys = text_ref[:, 0].reshape(128, 128)
                return dot_t(q, keys) * factor + bias_ref[...]
            keys = kv_ref[n // 2, n % 2, :, 0].reshape(1024, 128)
            return dot_t(q, keys) * factor

        highest = acc = None
        s = scores_of(0)
        for n in range(9):
            following = scores_of(n + 1) if n < 8 else None
            top = jnp.max(s, axis=-1, keepdims=True)
            if n > 0:
                top = jnp.maximum(highest, top)
            weights = jnp.exp2(s - top).astype(BF16)
            if n == 8:
                values = jnp.concatenate([text_ref[:, 1].reshape(128, 128), ones[:128]], axis=1)
            else:
                values = jnp.concatenate(
                    [kv_ref[n // 2, n % 2, :, 1].reshape(1024, 128), ones], axis=1
                )
            product = dot(weights, values)
            acc = product if n == 0 else acc * jnp.exp2(highest - top) + product
            highest = top
            s = following
        out = (acc[:, :HD] / acc[:, HD:]).astype(BF16)
        k = t * 2
        staged[k] = out[:128]
        staged[k + 1] = out[128:]
        deliver(k + 1).start()

        @pl.when(t > 0)
        def _():
            deliver(k).start()

        return 0

    lax.fori_loop(0, 8, tile, 0)
    own = pltpu.make_async_copy(staged.at[0], out_ref.at[:, columns], local_sem)
    own.start()
    own.wait()
    for k in range(1, 16):
        deliver(k).wait()


def local(
    enc_states, image_count, prompt_count, enc_gain, enc_gate, enc_up, enc_down, final_gain, w_in,
    mod_text, mod_video, w_kv_text, w_qkv, query_gain, key_gain, text_key_gain, video_states,
):
    vmem, hbm = pl.BlockSpec(memory_space=pltpu.VMEM), pl.BlockSpec(memory_space=pl.ANY)
    row = lambda v: v.reshape(1, -1)
    q, kv, text = pl.pallas_call(
        front_kernel,
        out_shape=[
            jax.ShapeDtypeStruct((2, 8, 128, 128), BF16),
            jax.ShapeDtypeStruct((4, 2, 8, 2, 128, 128), BF16),
            jax.ShapeDtypeStruct((4, 2, 32, 128), BF16),
        ],
        in_specs=[vmem] * 9 + [hbm] * 6,
        out_specs=[vmem] * 3,
        scratch_shapes=[
            pltpu.VMEM((128, D), BF16),
            pltpu.VMEM((256, D), BF16),
            pltpu.VMEM((256, D), BF16),
            pltpu.VMEM((256, D), BF16),
            pltpu.VMEM((128, D), BF16),
            pltpu.VMEM((2, D, 3 * HD), BF16),
            pltpu.VMEM((224, ED), BF16),
            pltpu.VMEM((224, ED), BF16),
            pltpu.VMEM((224, ED), BF16),
            pltpu.VMEM((64, D), BF16),
            pltpu.VMEM((D, 2 * HD), BF16),
            pltpu.VMEM((8, 128, 128), BF16),
            pltpu.VMEM((8, 2, 128, 128), BF16),
            pltpu.VMEM((4, 2, 8, 16, 512), BF16),
            pltpu.VMEM((128, ED), BF16),
            pltpu.VMEM((128, ED), BF16),
            pltpu.VMEM((4, 128, 1024), BF16),
            pltpu.VMEM((3, 128, 1024), BF16),
            pltpu.VMEM((8, 128, 128), BF16),
            pltpu.VMEM((7, 128, 128), BF16),
            pltpu.VMEM((128, 128), F32),
            pltpu.VMEM((128, 128), F32),
            pltpu.VMEM((4, 32, D + 128), BF16),
            pltpu.VMEM((3, 32, D + 128), BF16),
            pltpu.VMEM((8, 32, 512), BF16),
            pltpu.VMEM((7, 32, 512), BF16),
            pltpu.VMEM((32, 512), F32),
            pltpu.VMEM((32, 512), F32),
            pltpu.VMEM((8, 32, 384), BF16),
            pltpu.SemaphoreType.DMA((N_COPIES,)),
            pltpu.SemaphoreType.DMA((N_COPIES,)),
            pltpu.SemaphoreType.DMA((6,)),
        ],
        compiler_params=pltpu.CompilerParams(
            collective_id=0, has_side_effects=True, vmem_limit_bytes=56 * 2**20
        ),
        name="front",
    )(
        enc_states.reshape(16, 512), video_states, mod_video[0], mod_text[0], row(enc_gain),
        row(final_gain), row(query_gain), row(key_gain), row(text_key_gain),
        w_qkv[:, 0, :], enc_gate.T, enc_up.T, enc_down, w_in, w_kv_text[:, 0, :],
    )
    at = jnp.arange(128, dtype=jnp.int32)
    b, x, zz, r = at // 32, (at // 16) % 2, (at // 2) % 8, at % 2
    rows = 32 * b + 4 * zz + 2 * x + r
    live = jnp.where(rows < IMG_ROWS, rows < image_count[0], rows - IMG_ROWS < prompt_count[0])
    bias = jnp.where(live, 0.0, NEG).astype(F32).reshape(1, 128)
    return pl.pallas_call(
        attend_kernel,
        out_shape=jax.ShapeDtypeStruct((128, 2048), BF16),
        in_specs=[vmem] * 4,
        out_specs=vmem,
        scratch_shapes=[
            pltpu.VMEM((16, 128, 128), BF16),
            pltpu.SemaphoreType.DMA((16,)),
            pltpu.SemaphoreType.DMA((16,)),
            pltpu.SemaphoreType.DMA,
        ],
        compiler_params=pltpu.CompilerParams(
            collective_id=1, has_side_effects=True, vmem_limit_bytes=56 * 2**20
        ),
        name="attend",
    )(q, kv, text, bias)


def solution(mesh):
    placed = (
        P(("grp", "blk", "head"), None),
        P("grp"),
        P("grp"),
        P(),
        P(None, ("blk", "head")),
        P(None, ("blk", "head")),
        P(("blk", "head"), None),
        P(("blk", "head")),
        P(("blk", "head"), None),
        P("grp", None, None),
        P("grp", None, None),
        P(None, "head", None),
        P(None, "head", None),
        P(),
        P(),
        P(),
        P(("grp", "blk", "head"), None),
    )
    return jax.shard_map(
        local,
        mesh=mesh,
        in_specs=placed,
        out_specs=P(("grp", "blk", "head"), None),
        check_vma=False,
    )
```

time: 1610 us -> 157 us (0.10)
  waiting for transfers between devices: 1200 us -> 0 us
  blocking collectives: 196 us -> 0 us
  Pallas kernels: 0 us -> 151 us
  matrix products: 79.7 us -> 0 us
  starting transfers between devices: 56.8 us -> 0 us
  other arithmetic: 50.8 us -> 0.54 us
    psum x1 -> x0, waiting for transfers between devices: 658 us -> none  [local(): total_squares, refined = lax.psum((squares, partial_rows), ('blk', 'head'))]
    unnamed x5 -> x0, waiting for transfers between devices: 416 us -> none
    psum x1 -> x0, blocking collectives: 179 us -> none  [local(): total_squares, refined = lax.psum((squares, partial_rows), ('blk', 'head'))]
    pallas_call x0 -> x2, Pallas kernels: none -> 151 us  [the longest x1 116 us: local(): pl.pallas_call(front_kernel, out_shape=[jax.ShapeDtypeStruct((2, 8, 128,...]
    all_gather x2 -> x0, waiting for transfers between devices: 119 us -> none  [the longest x1 119 us: local(): piece = lax.all_gather(normed, ('blk', 'head'), axis=0, tiled=True)]
    dot_general x15 -> x0, matrix products: 79.7 us -> none  [the longest x5 32.7 us: attend_block(): jnp.einsum('qhe,khe->hqk', queries, keys, preferred_element_type=jnp.floa...]
    ppermute x3 -> x0, starting transfers between devices: 56.6 us -> none  [from_behind(): return lax.ppermute(block, axis, route)]
    reduce_sum x13 -> x0, other arithmetic: 42.2 us -> none  [the longest x5 34.6 us: attend_block(): total = total * factor + jnp.sum(weights, axis=-1)]
  transfers between devices with their start and end apart: 7 -> 0, of which waited for: 4 -> 0; matrix products, arithmetic and copies ran while one was open for 3% -> 0% of each run, Pallas kernels for 0% -> 0%
where the time goes in v1:
time: 157 us; the launch traced here: 156 us
  Pallas kernels  151 us (96%)
  local copies, waits for them, and re-layouts  3.22 us (2%)
    pallas_call x1, Pallas kernels, local(): pl.pallas_call(front_kernel, out_shape=[jax.ShapeDtypeStruct((2, 8, 128,...  116 us
    pallas_call x1, Pallas kernels, local(): pl.pallas_call(attend_kernel, out_shape=jax.ShapeDtypeStruct((128, 2048),...  35.1 us

profile of v1, /device:TPU:24, one launch (start us, length us, event | category | flops | bytes accessed | tf_op | source)
XLA Modules:
  0.0 155.7 jit_solution(1857643345204503727)
XLA Ops:
  1.3 0.5 select_select_fusion.bias_ref
  1.8 1.3 reshape.218.enc_own
  3.2 115.6 %front.1 = (bf16[2,8,128,128]{3,2,1,0:T(8,128)(2,1)}, bf16[4,2,8,2,128,128]{5,4,3,2,1,0:T(8,128)(2,1)}, bf16[4,2,32,128]{3,2,1,0:T(8,128)(2,1)}) custom-call(bf16[16,512]{1,0:T(8,128)(2,1)} %reshape.218.enc_own, bf16[128,3072]{1,0:T(8,128)(2,1)} %video.1, f32[2,3072]{1,0:T(2,128)} %bitcast.19, f32[2,3072]{1,0:T(2,128)} %bitcast.20, f32[1,4096]{1,0:T(1,128)} %bitcast.21, ...), custom_call_target="tpu_custom_call" | custom-call | tf_op jit(solution)/shard_map/front/pallas_call | solution.py:419
  118.7 35.1 %attend.1 = bf16[128,2048]{1,0:T(8,128)(2,1)} custom-call(bf16[2,8,128,128]{3,2,1,0:T(8,128)(2,1)} %get-tuple-element.8.q_ref, bf16[4,2,8,2,128,128]{5,4,3,2,1,0:T(8,128)(2,1)} %get-tuple-element.9.kv_ref, bf16[4,2,32,128]{3,2,1,0:T(8,128)(2,1)} %get-tuple-element.10.text_ref, f32[1,128]{1,0:T(1,128)} %select_select_fusion.bias_ref), custom_call_target="tpu_custom_call" | custom-call | tf_op jit(solution)/shard_map/attend/pallas_call | solution.py:476
  153.8 1.9 %copy.21 = bf16[128,2048]{1,0:T(8,128)(2,1)} copy(bf16[128,2048]{1,0:T(8,128)(2,1)} %attend.1) | data formatting | bytes 1048576

commit v2 on v0

v2 whole, which is shorter than its diff:
```python
import functools

import jax
import jax.numpy as jnp
from jax import lax
from jax.experimental import pallas as pl
from jax.experimental.pallas import tpu as pltpu
from jax.sharding import PartitionSpec as P

MESH = pl.DeviceIdType.MESH
EPS = 1e-06
NEG = -1e30
IMG_ROWS = 64
F32 = jnp.float32
BF16 = jnp.bfloat16
HD = 128
D = 3072
ED = 4096
STEP_CHUNKS = ((0, 1), (1, 2), (3, 2), (5, 2), (7, 1))
N_COPIES = 120


def dot(a, b):
    return jnp.dot(a, b, preferred_element_type=F32)


def dot_t(a, b):
    return lax.dot_general(a, b, (((1,), (1,)), ((), ())), preferred_element_type=F32)


def rms(values, gain):
    return values * lax.rsqrt(jnp.mean(values * values, axis=-1, keepdims=True) + EPS) * gain


class Links:
    def __init__(self, send, recv):
        self.send, self.recv, self.count, self.started = send, recv, 0, []

    def start(self, src, dst, device):
        copy = pltpu.make_async_remote_copy(
            src_ref=src,
            dst_ref=dst,
            send_sem=self.send.at[self.count],
            recv_sem=self.recv.at[self.count],
            device_id=device,
            device_id_type=MESH,
        )
        copy.start()
        self.count += 1
        assert self.count <= N_COPIES
        self.started.append(copy)
        return copy

    def drain(self):
        for copy in self.started:
            copy.wait_send()


def block_kernel(
    image_count, prompt_count,
    enc_own, video, mod_video, mod_text, enc_gain, final_gain, query_gain, key_gain, text_gain,
    w_qkv, gate_t, up_t, down, w_in, w_kv,
    out_ref,
    q_ref, kv_ref, text_ref, acc_ref, top_ref, staged,
    tok0, tok1, tok2, tok3, tok4, w_two, g_v, u_v, d_v, wi_v, wk_v,
    xq, xkv, granules, rows_v, normed_v, term_a, r_term_a, term_b, r_term_b, half_f, half_b,
    r_half, sum_b, r_sum_b, part, r_part,
    gain_v, proj, r_proj, proj_z, r_projz, cond, cond_mod,
    send, recv, out_send, out_recv, local_sem,
):
    g, y, h = lax.axis_index("grp"), lax.axis_index("blk"), lax.axis_index("head")
    z, X = h // 2, h % 2
    core = g % 2
    z_at = lambda dz: (g, y, ((z + dz) % 8) * 2 + X)
    y_at = lambda dy: (g, (y + dy) % 4, h)
    x_at = (g, y, z * 2 + (1 - X))
    w_at = ((g + 2) % 4, y, z * 2 + (1 - X))
    core_at = (g + 1 - 2 * core, y, h)

    def owner(k):
        c, x_rel = k % 8, k // 8
        offset = (c % 2) * (8 - (c + 1) // 2) + (1 - c % 2) * (c // 2)
        return (g, y, ((z + offset) % 8) * 2 + (X + x_rel) % 2)

    peers = [owner(k) for k in range(1, 16)] + [y_at(i) for i in range(1, 4)] + [w_at, core_at]

    loads = [
        pltpu.make_async_copy(src, dst, local_sem.at[i])
        for i, (src, dst) in enumerate(
            [(w_qkv, w_two.at[0]), (gate_t, g_v), (up_t, u_v), (down, d_v), (w_in, wi_v.at[X]), (w_kv, wk_v)]
        )
    ]
    for load in loads:
        load.start()

    barrier = pltpu.get_barrier_semaphore()
    for peer in peers:
        pl.semaphore_signal(barrier, inc=1, device_id=peer, device_id_type=MESH)
    pl.semaphore_wait(barrier, len(peers))

    links = Links(send, recv)
    toks = [tok0, tok1, tok2, tok3, tok4]
    flight = {}

    def landed(name):
        for copy in flight[name]:
            copy.wait_recv()

    seen = set()

    def once(name):
        if name not in seen:
            seen.add(name)
            landed(name)

    def to_y(src, dst):
        return [links.start(src((y + i) % 4), dst(i), y_at(i)) for i in (1, 3, 2)]

    def to_z(src, dst):
        return [links.start(src((z + i) % 8), dst(i), z_at(i)) for i in (1, 7, 2, 6, 3, 5, 4)]

    def modulate_video():
        scale, shift = 1.0 + mod_video[1:2, :], mod_video[0:1, :]

        def modulate(i, _):
            at = pl.ds(pl.multiple_of(i * 16, 16), 16)
            v = video[at, :].astype(F32)
            c = v - jnp.mean(v, axis=-1, keepdims=True)
            n = c * lax.rsqrt(jnp.mean(c * c, axis=-1, keepdims=True) + EPS)
            tok0[at, :] = (n * scale + shift).astype(BF16)
            return 0

        lax.fori_loop(0, 8, modulate, 0)

    def ring(step, part):
        at, low, high = pl.ds(64 * part, 64), 64 * part, 128 + 64 * part
        back = tok0.at[at] if step == 1 else toks[step - 1].at[pl.ds(high, 64)]
        copies = []
        if step < 4 or part == 0:
            copies.append(links.start(toks[step - 1].at[at], toks[step].at[at], z_at(1)))
        if step < 4:
            copies.append(links.start(back, toks[step].at[pl.ds(high, 64)], z_at(7)))
        elif part == 1:
            copies.append(links.start(back, tok4.at[at], z_at(7)))
        flight["tok", step, part] = copies

    def arrive(step, part):
        landed(("tok", step, part))
        if step < 4:
            ring(step + 1, part)

    half = pl.ds(pl.multiple_of(core * (D // 2), D // 2), D // 2)

    def weights_x():
        flight["w_half"] = [links.start(w_qkv.at[half], w_two.at[1, half], w_at)]

    def weights_core():
        landed("w_half")
        flight["w_core"] = [links.start(w_two.at[1, half], w_two.at[1, half], core_at)]

    def project(step, which):
        first, count = STEP_CHUNKS[step]
        mixed = dot(toks[step][...], w_two[which])
        q = rms(mixed[:, :HD], query_gain[...]).astype(BF16)
        k = rms(mixed[:, HD : 2 * HD], key_gain[...]).astype(BF16)
        v = mixed[:, 2 * HD :].astype(BF16)
        for i in range(count):
            at = slice(i * 128, (i + 1) * 128)
            if which == 0:
                q_ref[0, first + i] = q[at]
                kv_ref[0, 0, first + i, 0] = k[at]
                kv_ref[0, 0, first + i, 1] = v[at]
            else:
                xq[first + i] = q[at]
                xkv[first + i, 0] = k[at]
                xkv[first + i, 1] = v[at]

    def spread(step, x_rel):
        chunks = pl.ds(*STEP_CHUNKS[step])
        if x_rel:
            landed(("x", step))
        mine = kv_ref.at[0, x_rel, chunks]
        flight["kv", step, x_rel] = [
            links.start(mine, kv_ref.at[3, x_rel, chunks], y_at(1)),
            links.start(mine, kv_ref.at[1, x_rel, chunks], y_at(3)),
        ]

    def relay(step, x_rel):
        chunks = pl.ds(*STEP_CHUNKS[step])
        landed(("kv", step, x_rel))
        far = kv_ref.at[2, x_rel, chunks]
        flight["far", step, x_rel] = [
            links.start(kv_ref.at[3, x_rel, chunks, 0], far.at[:, 0], y_at(1)),
            links.start(kv_ref.at[1, x_rel, chunks, 1], far.at[:, 1], y_at(3)),
        ]

    def own_head(step):
        if step == 0:
            loads[0].wait()
        project(step, 0)

    def other_head(step):
        once("w_core")
        chunks = pl.ds(*STEP_CHUNKS[step])
        project(step, 1)
        flight["q", step] = [links.start(xq.at[chunks], q_ref.at[1, chunks], x_at)]
        flight["x", step] = [links.start(xkv.at[chunks], kv_ref.at[0, 1, chunks], x_at)]

    def enc_z():
        rows = enc_own[...].astype(F32)
        pieces = [rows[:, 512 * j : 512 * j + 512] for j in range(8)]
        granules[y, X, z] = jnp.concatenate(pieces, axis=0).astype(BF16)
        flight["enc_z"] = to_z(lambda _: granules.at[y, X, z], lambda _: granules.at[y, X, z])

    def enc_x():
        landed("enc_z")
        flight["enc_x"] = [links.start(granules.at[y, X], granules.at[y, X], x_at)]

    def enc_y():
        landed("enc_x")
        mine = granules.at[y]
        flight["enc_y"] = [links.start(mine, mine, y_at(1)), links.start(mine, mine, y_at(3))]

    def enc_far():
        landed("enc_y")
        low, high = granules.at[(y + 3) % 4, 0], granules.at[(y + 1) % 4, 1]
        flight["enc_far"] = [links.start(low, low, y_at(1)), links.start(high, high, y_at(3))]

    def gains_x():
        gain = jnp.concatenate([final_gain[...], jnp.zeros((1, 64), F32)], axis=1)
        gain_v[X] = jnp.broadcast_to(gain, (8, 128))
        flight["gains"] = [
            links.start(gain_v.at[X], gain_v.at[X], x_at),
            links.start(w_in, wi_v.at[X], x_at),
        ]

    def feed_forward():
        landed("enc_far")
        out_at = lax.broadcasted_iota(jnp.int32, (256, 256), 0)
        in_at = lax.broadcasted_iota(jnp.int32, (256, 256), 1)
        source = out_at % 32 // 2 * 16 + out_at // 32 * 2 + out_at % 2
        order = (in_at == source).astype(F32).astype(BF16)
        for b in range(4):
            ordered = dot(order, granules[b].reshape(256, 512)).astype(BF16)
            for j in range(8):
                for x in (0, 1):
                    rows_v[64 * x + 16 * b : 64 * x + 16 * b + 16, 512 * j : 512 * j + 512] = ordered[
                        32 * j + 16 * x : 32 * j + 16 * x + 16
                    ]

        def normalize(i, _):
            at = pl.ds(pl.multiple_of(i * 16, 16), 16)
            v = rows_v[at, :].astype(F32)
            normed_v[at, :] = rms(v, enc_gain[...]).astype(BF16)
            return 0

        lax.fori_loop(0, 8, normalize, 0)
        loads[1].wait()
        loads[2].wait()
        gate = dot_t(normed_v[...], g_v[...])
        upward = dot_t(normed_v[...], u_v[...])
        hidden = (gate / (1.0 + jnp.exp(-gate)) * upward).astype(BF16)
        loads[3].wait()
        for b in range(4):
            product = dot(hidden, d_v[:, 1024 * b : 1024 * b + 1024]).astype(BF16)
            term_a[b] = product[:, :512]
            term_b[0, b] = product[:64, 512:]
            term_b[1, b] = product[64:, 512:]
        flight["sum_a"] = to_y(lambda b: term_a.at[b], lambda i: r_term_a.at[i - 1])
        flight["sum_b"] = [links.start(term_b.at[1 - X], r_term_b, x_at)]

    def sum_xa():
        landed("sum_a")
        total = term_a[y].astype(F32)
        for i in range(3):
            total = total + r_term_a[i].astype(F32)
        for x in (0, 1):
            half_f[x] = total[64 * x : 64 * x + 64]
            half_b[x] = total[64 * x : 64 * x + 64].astype(BF16)
        flight["sum_xa"] = [links.start(half_b.at[1 - X], r_half, x_at)]

    def sum_yb():
        landed("sum_b")
        for b in range(4):
            sum_b[b] = (term_b[X, b].astype(F32) + r_term_b[b].astype(F32)).astype(BF16)
        flight["sum_yb"] = to_y(lambda b: sum_b.at[b], lambda i: r_sum_b.at[i - 1])

    def sum_z():
        landed("sum_xa")
        landed("sum_yb")
        total = half_f[X] + r_half[...].astype(F32)
        for i in range(4):
            part[i] = total[:, 128 * i : 128 * i + 128].astype(BF16)
        total = sum_b[y].astype(F32)
        for i in range(3):
            total = total + r_sum_b[i].astype(F32)
        for i in range(4):
            part[4 + i] = total[:, 128 * i : 128 * i + 128].astype(BF16)
        flight["sum_z"] = to_z(lambda b: part.at[b], lambda i: r_part.at[i - 1])

    def refine():
        landed("sum_z")
        total = part[z].astype(F32)
        for i in range(7):
            total = total + r_part[i].astype(F32)
        column = pl.multiple_of(y * 1024 + z * 128, 128)
        own_rows = pl.ds(pl.multiple_of(X * 64, 64), 64)
        enc_out = total + rows_v[own_rows, pl.ds(column, 128)].astype(F32)
        squares = jnp.sum(enc_out * enc_out, axis=-1, keepdims=True)
        landed("gains")
        gain = jnp.concatenate([gain_v[0][:1, :64], gain_v[1][:1, :64]], axis=1)
        scaled = (enc_out * gain).astype(BF16)
        loads[4].wait()
        wide = jnp.broadcast_to(squares, (64, 128)).astype(BF16)
        for b in range(4):
            proj[b, :, D:] = wide[16 * b : 16 * b + 16]
        for i in range(6):
            weights = wi_v[:, :, 512 * i : 512 * i + 512].reshape(128, 512)
            product = dot(scaled, weights).astype(BF16)
            for b in range(4):
                proj[b, :, 512 * i : 512 * i + 512] = product[16 * b : 16 * b + 16]
        flight["ref_y"] = to_y(lambda b: proj.at[b], lambda i: r_proj.at[i - 1])

    def refine_z():
        landed("ref_y")
        total = proj[y].astype(F32)
        for i in range(3):
            total = total + r_proj[i].astype(F32)
        for i in range(8):
            proj_z[i, :, :384] = total[:, 384 * i : 384 * i + 384].astype(BF16)
            proj_z[i, :, 384:] = total[:, D:].astype(BF16)
        flight["ref_z"] = to_z(lambda b: proj_z.at[b], lambda i: r_projz.at[i - 1])

    def refine_all():
        landed("ref_z")
        total = proj_z[z].astype(F32)
        for i in range(7):
            total = total + r_projz[i].astype(F32)
        cond[z] = (total[:, :384] * lax.rsqrt(total[:, 384:385] / ED + EPS)).astype(BF16)
        flight["cond"] = to_z(lambda _: cond.at[z], lambda _: cond.at[z])

    def modulate_x():
        landed("cond")
        total = jnp.zeros((16, 1), F32)
        for i in range(8):
            total = total + jnp.sum(cond[i].astype(F32), axis=-1, keepdims=True)
        mean = total / D
        total = jnp.zeros((16, 1), F32)
        for i in range(8):
            c = cond[i].astype(F32) - mean
            total = total + jnp.sum(c * c, axis=-1, keepdims=True)
        inverse = lax.rsqrt(total / D + EPS)
        for i in range(8):
            at = slice(384 * i, 384 * i + 384)
            c = (cond[i].astype(F32) - mean) * inverse
            cond_mod[X, :, at] = (c * (1.0 + mod_text[1:2, at]) + mod_text[0:1, at]).astype(BF16)
        flight["cond_mod"] = [links.start(cond_mod.at[X], cond_mod.at[X], x_at)]

    def text():
        landed("cond_mod")
        loads[5].wait()
        text_kv = dot(cond_mod[...].reshape(32, D), wk_v[...])
        text_ref[y, 0] = rms(text_kv[:, :HD], text_gain[...]).astype(BF16)
        text_ref[y, 1] = text_kv[:, HD:].astype(BF16)
        flight["text"] = to_y(lambda _: text_ref.at[y], lambda _: text_ref.at[y])

    factor = HD ** (-0.5) * 1.4426950408889634

    def dead_bias():
        at = lax.broadcasted_iota(jnp.int32, (1, 128), 1)
        row = at // 32 * 32 + at // 2 % 8 * 4 + at // 16 % 2 * 2 + at % 2
        end = jnp.where(row < IMG_ROWS, image_count[0], IMG_ROWS + prompt_count[0])
        return jnp.where(row < end, 0.0, NEG)

    def attend(i, tiles, fresh, last):
        q = q_ref[:, i].reshape(256, 128)
        tiles = list(tiles) + (["text"] if last else [])

        def scores_of(n):
            if n == "text":
                return dot_t(q, text_ref[:, 0].reshape(128, 128)) * factor + dead_bias()
            return dot_t(q, kv_ref[:, :, n, 0].reshape(1024, 128)) * factor

        def values_of(n):
            if n == "text":
                v = text_ref[:, 1].reshape(128, 128)
            else:
                v = kv_ref[:, :, n, 1].reshape(1024, 128)
            return jnp.concatenate([v, jnp.ones(v.shape, BF16)], axis=1)

        highest = acc = None
        if not fresh:
            highest, acc = top_ref[i][:, :1], acc_ref[i]
        s = scores_of(tiles[0])
        for at, n in enumerate(tiles):
            following = scores_of(tiles[at + 1]) if at + 1 < len(tiles) else None
            top = jnp.max(s, axis=-1, keepdims=True)
            if highest is not None:
                top = jnp.maximum(highest, top)
            product = dot(jnp.exp2(s - top).astype(BF16), values_of(n))
            acc = product if highest is None else acc * jnp.exp2(highest - top) + product
            highest, s = top, following
        if not last:
            top_ref[i] = jnp.broadcast_to(highest, (256, 128))
            acc_ref[i] = acc
            return
        out = (acc[:, :HD] / acc[:, HD:]).astype(BF16)
        staged[i] = out[:128]
        staged[8 + i] = out[128:]
        deliver(8 + i).start()

        @pl.when(i > 0)
        def _():
            deliver(i).start()

    def queries(first, end, tiles, fresh, last=False):
        def body(i, _):
            attend(end - 1 - i, tiles, fresh, last)
            return 0

        lax.fori_loop(0, end - first, body, 0)

    def attend_to(first, end, key_first, key_end, last=False):
        for step, (chunk, _) in enumerate(STEP_CHUNKS):
            if chunk < key_end:
                once(("far", step, 0))
                once(("far", step, 1))
            if chunk < end:
                once(("q", step))
        if last:
            once("text")
        queries(first, end, range(key_first, key_end), key_first == 0, last)

    columns = pl.ds(pl.multiple_of(h * 128, 128), 128)

    def deliver(k):
        return pltpu.make_async_remote_copy(
            src_ref=staged.at[k],
            dst_ref=out_ref.at[:, columns],
            send_sem=out_send.at[k],
            recv_sem=out_recv.at[k],
            device_id=owner(k),
            device_id_type=MESH,
        )

    def finish():
        own = pltpu.make_async_copy(staged.at[0], out_ref.at[:, columns], local_sem.at[6])
        own.start()
        own.wait()
        links.drain()
        for k in range(1, 16):
            deliver(k).wait()

    stages = locals()
    for name, *step in PLAN:
        stages[name](*step)


PLAN = (
    ("enc_z",), ("modulate_video",), ("ring", 1, 0), ("own_head", 0), ("spread", 0, 0),
    ("ring", 1, 1), ("weights_x",), ("gains_x",), ("enc_x",), ("relay", 0, 0), ("enc_y",),
    ("enc_far",), ("arrive", 1, 0), ("arrive", 1, 1), ("own_head", 1), ("spread", 1, 0),
    ("feed_forward",), ("relay", 1, 0), ("weights_core",), ("other_head", 1), ("sum_yb",),
    ("sum_xa",), ("arrive", 2, 0), ("arrive", 2, 1), ("own_head", 2), ("spread", 2, 0),
    ("other_head", 0), ("other_head", 2), ("sum_z",), ("spread", 1, 1), ("relay", 2, 0),
    ("spread", 0, 1), ("spread", 2, 1), ("relay", 1, 1), ("relay", 0, 1), ("refine",),
    ("attend_to", 0, 3, 0, 3), ("relay", 2, 1), ("arrive", 3, 0), ("arrive", 3, 1),
    ("other_head", 3), ("own_head", 3), ("spread", 3, 0), ("refine_z",), ("attend_to", 3, 5, 0, 5),
    ("spread", 3, 1), ("attend_to", 5, 6, 0, 5), ("relay", 3, 0), ("attend_to", 0, 3, 3, 5),
    ("refine_all",), ("arrive", 4, 0), ("relay", 3, 1), ("arrive", 4, 1), ("own_head", 4),
    ("spread", 4, 0), ("other_head", 4), ("attend_to", 6, 7, 0, 5), ("modulate_x",),
    ("attend_to", 5, 7, 5, 7), ("spread", 4, 1), ("relay", 4, 0), ("attend_to", 7, 8, 0, 7),
    ("text",), ("relay", 4, 1), ("attend_to", 0, 5, 5, 7), ("attend_to", 0, 8, 7, 8, True),
    ("finish",),
)


def local(
    enc_states, image_count, prompt_count, enc_gain, enc_gate, enc_up, enc_down, final_gain, w_in,
    mod_text, mod_video, w_kv_text, w_qkv, query_gain, key_gain, text_key_gain, video_states,
):
    vmem, hbm = pl.BlockSpec(memory_space=pltpu.VMEM), pl.BlockSpec(memory_space=pl.ANY)
    smem = pl.BlockSpec(memory_space=pltpu.SMEM)
    row = lambda v: v.reshape(1, -1)
    return pl.pallas_call(
        block_kernel,
        out_shape=jax.ShapeDtypeStruct((128, 2048), BF16),
        in_specs=[smem] * 2 + [vmem] * 9 + [hbm] * 6,
        out_specs=vmem,
        scratch_shapes=[
            pltpu.VMEM((2, 8, 128, 128), BF16),
            pltpu.VMEM((4, 2, 8, 2, 128, 128), BF16),
            pltpu.VMEM((4, 2, 32, 128), BF16),
            pltpu.VMEM((8, 256, 256), F32),
            pltpu.VMEM((8, 256, 128), F32),
            pltpu.VMEM((16, 128, 128), BF16),
            pltpu.VMEM((128, D), BF16),
            pltpu.VMEM((256, D), BF16),
            pltpu.VMEM((256, D), BF16),
            pltpu.VMEM((256, D), BF16),
            pltpu.VMEM((128, D), BF16),
            pltpu.VMEM((2, D, 3 * HD), BF16),
            pltpu.VMEM((224, ED), BF16),
            pltpu.VMEM((224, ED), BF16),
            pltpu.VMEM((224, ED), BF16),
            pltpu.VMEM((2, 64, D), BF16),
            pltpu.VMEM((D, 2 * HD), BF16),
            pltpu.VMEM((8, 128, 128), BF16),
            pltpu.VMEM((8, 2, 128, 128), BF16),
            pltpu.VMEM((4, 2, 8, 16, 512), BF16),
            pltpu.VMEM((128, ED), BF16),
            pltpu.VMEM((128, ED), BF16),
            pltpu.VMEM((4, 128, 512), BF16),
            pltpu.VMEM((3, 128, 512), BF16),
            pltpu.VMEM((2, 4, 64, 512), BF16),
            pltpu.VMEM((4, 64, 512), BF16),
            pltpu.VMEM((2, 64, 512), F32),
            pltpu.VMEM((2, 64, 512), BF16),
            pltpu.VMEM((64, 512), BF16),
            pltpu.VMEM((4, 64, 512), BF16),
            pltpu.VMEM((3, 64, 512), BF16),
            pltpu.VMEM((8, 64, 128), BF16),
            pltpu.VMEM((7, 64, 128), BF16),
            pltpu.VMEM((2, 8, 128), F32),
            pltpu.VMEM((4, 16, D + 128), BF16),
            pltpu.VMEM((3, 16, D + 128), BF16),
            pltpu.VMEM((8, 16, 512), BF16),
            pltpu.VMEM((7, 16, 512), BF16),
            pltpu.VMEM((8, 16, 384), BF16),
            pltpu.VMEM((2, 16, D), BF16),
            pltpu.SemaphoreType.DMA((N_COPIES,)),
            pltpu.SemaphoreType.DMA((N_COPIES,)),
            pltpu.SemaphoreType.DMA((16,)),
            pltpu.SemaphoreType.DMA((16,)),
            pltpu.SemaphoreType.DMA((7,)),
        ],
        compiler_params=pltpu.CompilerParams(
            collective_id=0, has_side_effects=True, vmem_limit_bytes=58 * 2**20
        ),
        name="block",
    )(
        image_count, prompt_count, enc_states, video_states, mod_video[0], mod_text[0], row(enc_gain),
        row(final_gain), row(query_gain), row(key_gain), row(text_key_gain),
        w_qkv[:, 0, :], enc_gate.T, enc_up.T, enc_down, w_in, w_kv_text[:, 0, :],
    )


def solution(mesh):
    placed = (
        P(("grp", "blk", "head"), None),
        P("grp"),
        P("grp"),
        P(),
        P(None, ("blk", "head")),
        P(None, ("blk", "head")),
        P(("blk", "head"), None),
        P(("blk", "head")),
        P(("blk", "head"), None),
        P("grp", None, None),
        P("grp", None, None),
        P(None, "head", None),
        P(None, "head", None),
        P(),
        P(),
        P(),
        P(("grp", "blk", "head"), None),
    )
    return jax.shard_map(
        local,
        mesh=mesh,
        in_specs=placed,
        out_specs=P(("grp", "blk", "head"), None),
        check_vma=False,
    )
```

time: 1610 us -> 143 us (0.09)
  waiting for transfers between devices: 1200 us -> 0 us
  blocking collectives: 196 us -> 0 us
  Pallas kernels: 0 us -> 138 us
  matrix products: 79.7 us -> 0 us
  starting transfers between devices: 56.8 us -> 0 us
  other arithmetic: 50.8 us -> 0 us
    psum x1 -> x0, waiting for transfers between devices: 658 us -> none  [local(): total_squares, refined = lax.psum((squares, partial_rows), ('blk', 'head'))]
    unnamed x5 -> x0, waiting for transfers between devices: 416 us -> none
    psum x1 -> x0, blocking collectives: 179 us -> none  [local(): total_squares, refined = lax.psum((squares, partial_rows), ('blk', 'head'))]
    pallas_call x0 -> x1, Pallas kernels: none -> 138 us  [local(): pl.pallas_call(block_kernel, out_shape=jax.ShapeDtypeStruct((128, 2048),...]
    all_gather x2 -> x0, waiting for transfers between devices: 119 us -> none  [the longest x1 119 us: local(): piece = lax.all_gather(normed, ('blk', 'head'), axis=0, tiled=True)]
    dot_general x15 -> x0, matrix products: 79.7 us -> none  [the longest x5 32.7 us: attend_block(): jnp.einsum('qhe,khe->hqk', queries, keys, preferred_element_type=jnp.floa...]
    ppermute x3 -> x0, starting transfers between devices: 56.6 us -> none  [from_behind(): return lax.ppermute(block, axis, route)]
    reduce_sum x13 -> x0, other arithmetic: 42.2 us -> none  [the longest x5 34.6 us: attend_block(): total = total * factor + jnp.sum(weights, axis=-1)]
  transfers between devices with their start and end apart: 7 -> 0, of which waited for: 4 -> 0; matrix products, arithmetic and copies ran while one was open for 3% -> 0% of each run, Pallas kernels for 0% -> 0%
where the time goes in v2:
time: 143 us; the launch traced here: 141 us
  Pallas kernels  138 us (97%)
  local copies, waits for them, and re-layouts  1.88 us (1%)
    pallas_call x1, Pallas kernels, local(): pl.pallas_call(block_kernel, out_shape=jax.ShapeDtypeStruct((128, 2048),...  138 us

profile of v2, /device:TPU:24, one launch (start us, length us, event | category | flops | bytes accessed | tf_op | source)
XLA Modules:
  0.0 141.1 jit_solution(15361787034573541645)
XLA Ops:
  1.3 138.0 %block.1 = bf16[128,2048]{1,0:T(8,128)(2,1)} custom-call(s32[1]{0:T(128)S(6)} %copy.19.image_count, s32[1]{0:T(128)S(6)} %copy.20.prompt_count, bf16[2,4096]{1,0:T(2,128)(2,1)} %enc_own.1, bf16[128,3072]{1,0:T(8,128)(2,1)} %video.1, f32[2,3072]{1,0:T(2,128)} %bitcast.15, f32[2,3072]{1,0:T(2,128)} %bitcast.16, f32[1,4096]{1,0:T(1,128)} %bitcast.17, ...), custom_call_target="tpu_custom_call" | custom-call | tf_op jit(solution)/shard_map/block/pallas_call | solution.py:485
  139.3 1.9 %copy.21 = bf16[128,2048]{1,0:T(8,128)(2,1)} copy(bf16[128,2048]{1,0:T(8,128)(2,1)} %block.1) | data formatting | bytes 1048576

commit v3 on v2

--- a/solution.py
+++ b/solution.py
@@ -17,7 +17,7 @@
 D = 3072
 ED = 4096
 STEP_CHUNKS = ((0, 1), (1, 2), (3, 2), (5, 2), (7, 1))
-N_COPIES = 120
+N_COPIES = 128
 
 
 def dot(a, b):
@@ -70,11 +70,12 @@
 ):
     g, y, h = lax.axis_index("grp"), lax.axis_index("blk"), lax.axis_index("head")
     z, X = h // 2, h % 2
-    core = g % 2
+    x_lo, core = g // 2, g % 2
     z_at = lambda dz: (g, y, ((z + dz) % 8) * 2 + X)
     y_at = lambda dy: (g, (y + dy) % 4, h)
     x_at = (g, y, z * 2 + (1 - X))
     w_at = ((g + 2) % 4, y, z * 2 + (1 - X))
+    beside_at = ((g + 2) % 4, y, h)
     core_at = (g + 1 - 2 * core, y, h)
 
     def owner(k):
@@ -82,7 +83,7 @@
         offset = (c % 2) * (8 - (c + 1) // 2) + (1 - c % 2) * (c // 2)
         return (g, y, ((z + offset) % 8) * 2 + (X + x_rel) % 2)
 
-    peers = [owner(k) for k in range(1, 16)] + [y_at(i) for i in range(1, 4)] + [w_at, core_at]
+    peers = [owner(k) for k in range(1, 16)] + [y_at(i) for i in range(1, 4)] + [w_at, beside_at, core_at]
 
     loads = [
         pltpu.make_async_copy(src, dst, local_sem.at[i])
@@ -119,18 +120,18 @@
     def to_z(src, dst):
         return [links.start(src((z + i) % 8), dst(i), z_at(i)) for i in (1, 7, 2, 6, 3, 5, 4)]
 
-    def modulate_video():
+    def modulate_video(part):
         scale, shift = 1.0 + mod_video[1:2, :], mod_video[0:1, :]
 
         def modulate(i, _):
-            at = pl.ds(pl.multiple_of(i * 16, 16), 16)
+            at = pl.ds(pl.multiple_of(64 * part + i * 16, 16), 16)
             v = video[at, :].astype(F32)
             c = v - jnp.mean(v, axis=-1, keepdims=True)
             n = c * lax.rsqrt(jnp.mean(c * c, axis=-1, keepdims=True) + EPS)
             tok0[at, :] = (n * scale + shift).astype(BF16)
             return 0
 
-        lax.fori_loop(0, 8, modulate, 0)
+        lax.fori_loop(0, 4, modulate, 0)
 
     def ring(step, part):
         at, low, high = pl.ds(64 * part, 64), 64 * part, 128 + 64 * part
@@ -149,14 +150,25 @@
         if step < 4:
             ring(step + 1, part)
 
-    half = pl.ds(pl.multiple_of(core * (D // 2), D // 2), D // 2)
+    def quarter(x_lo):
+        return pl.ds(pl.multiple_of((2 * x_lo + core) * (D // 4), D // 4), D // 4)
+
+    other = w_two.at[1]
+    here, there = quarter(x_lo), quarter(1 - x_lo)
 
     def weights_x():
-        flight["w_half"] = [links.start(w_qkv.at[half], w_two.at[1, half], w_at)]
+        flight["w_x"] = [links.start(w_qkv.at[there], other.at[there], w_at)]
+
+    def weights_l():
+        landed("w_x")
+        flight["w_l"] = [
+            links.start(other.at[here], other.at[here], beside_at),
+            links.start(other.at[here], other.at[here], core_at),
+        ]
 
     def weights_core():
-        landed("w_half")
-        flight["w_core"] = [links.start(w_two.at[1, half], w_two.at[1, half], core_at)]
+        landed("w_l")
+        flight["w_core"] = [links.start(other.at[there], other.at[there], core_at)]
 
     def project(step, which):
         first, count = STEP_CHUNKS[step]
@@ -226,13 +238,20 @@
         low, high = granules.at[(y + 3) % 4, 0], granules.at[(y + 1) % 4, 1]
         flight["enc_far"] = [links.start(low, low, y_at(1)), links.start(high, high, y_at(3))]
 
+    w_in_half = pl.ds(pl.multiple_of(32 * core, 32), 32)
+
     def gains_x():
         gain = jnp.concatenate([final_gain[...], jnp.zeros((1, 64), F32)], axis=1)
         gain_v[X] = jnp.broadcast_to(gain, (8, 128))
         flight["gains"] = [
             links.start(gain_v.at[X], gain_v.at[X], x_at),
-            links.start(w_in, wi_v.at[X], x_at),
+            links.start(w_in.at[w_in_half], wi_v.at[X, w_in_half], x_at),
         ]
+
+    def gains_core():
+        landed("gains")
+        half = wi_v.at[1 - X, w_in_half]
+        flight["gains_core"] = [links.start(half, half, core_at)]
 
     def feed_forward():
         landed("enc_far")
@@ -307,7 +326,7 @@
         own_rows = pl.ds(pl.multiple_of(X * 64, 64), 64)
         enc_out = total + rows_v[own_rows, pl.ds(column, 128)].astype(F32)
         squares = jnp.sum(enc_out * enc_out, axis=-1, keepdims=True)
-        landed("gains")
+        landed("gains_core")
         gain = jnp.concatenate([gain_v[0][:1, :64], gain_v[1][:1, :64]], axis=1)
         scaled = (enc_out * gain).astype(BF16)
         loads[4].wait()
@@ -457,21 +476,21 @@
 
 
 PLAN = (
-    ("enc_z",), ("modulate_video",), ("ring", 1, 0), ("own_head", 0), ("spread", 0, 0),
-    ("ring", 1, 1), ("weights_x",), ("gains_x",), ("enc_x",), ("relay", 0, 0), ("enc_y",),
-    ("enc_far",), ("arrive", 1, 0), ("arrive", 1, 1), ("own_head", 1), ("spread", 1, 0),
-    ("feed_forward",), ("relay", 1, 0), ("weights_core",), ("other_head", 1), ("sum_yb",),
-    ("sum_xa",), ("arrive", 2, 0), ("arrive", 2, 1), ("own_head", 2), ("spread", 2, 0),
-    ("other_head", 0), ("other_head", 2), ("sum_z",), ("spread", 1, 1), ("relay", 2, 0),
-    ("spread", 0, 1), ("spread", 2, 1), ("relay", 1, 1), ("relay", 0, 1), ("refine",),
-    ("attend_to", 0, 3, 0, 3), ("relay", 2, 1), ("arrive", 3, 0), ("arrive", 3, 1),
-    ("other_head", 3), ("own_head", 3), ("spread", 3, 0), ("refine_z",), ("attend_to", 3, 5, 0, 5),
-    ("spread", 3, 1), ("attend_to", 5, 6, 0, 5), ("relay", 3, 0), ("attend_to", 0, 3, 3, 5),
-    ("refine_all",), ("arrive", 4, 0), ("relay", 3, 1), ("arrive", 4, 1), ("own_head", 4),
-    ("spread", 4, 0), ("other_head", 4), ("attend_to", 6, 7, 0, 5), ("modulate_x",),
-    ("attend_to", 5, 7, 5, 7), ("spread", 4, 1), ("relay", 4, 0), ("attend_to", 7, 8, 0, 7),
-    ("text",), ("relay", 4, 1), ("attend_to", 0, 5, 5, 7), ("attend_to", 0, 8, 7, 8, True),
-    ("finish",),
+    ("enc_z",), ("modulate_video", 0), ("ring", 1, 0), ("modulate_video", 1), ("own_head", 0),
+    ("ring", 1, 1), ("weights_x",), ("enc_x",), ("spread", 0, 0), ("enc_y",), ("arrive", 1, 0),
+    ("weights_l",), ("enc_far",), ("arrive", 1, 1), ("own_head", 1), ("spread", 1, 0),
+    ("relay", 1, 0), ("feed_forward",), ("weights_core",), ("arrive", 2, 0), ("other_head", 0),
+    ("other_head", 1), ("arrive", 2, 1), ("own_head", 2), ("spread", 2, 0), ("sum_yb",),
+    ("relay", 0, 0), ("other_head", 2), ("spread", 0, 1), ("spread", 1, 1), ("sum_xa",),
+    ("gains_x",), ("spread", 2, 1), ("relay", 2, 0), ("relay", 0, 1), ("sum_z",), ("gains_core",),
+    ("relay", 1, 1), ("arrive", 3, 0), ("arrive", 3, 1), ("own_head", 3), ("relay", 2, 1),
+    ("other_head", 3), ("refine",), ("attend_to", 0, 3, 0, 3), ("spread", 3, 0),
+    ("attend_to", 0, 3, 3, 5), ("refine_z",), ("arrive", 4, 0), ("spread", 3, 1), ("arrive", 4, 1),
+    ("own_head", 4), ("spread", 4, 0), ("other_head", 4), ("attend_to", 6, 7, 0, 5),
+    ("attend_to", 5, 6, 0, 5), ("relay", 3, 1), ("relay", 3, 0), ("refine_all",), ("relay", 4, 0),
+    ("attend_to", 3, 5, 0, 5), ("modulate_x",), ("attend_to", 5, 7, 5, 7), ("spread", 4, 1),
+    ("attend_to", 7, 8, 0, 7), ("text",), ("relay", 4, 1), ("attend_to", 0, 5, 5, 7),
+    ("attend_to", 0, 8, 7, 8, True), ("finish",),
 )
 
 

time: 143 us -> 121 us (0.85); the launches traced: 141 us -> 121 us
  Pallas kernels: 138 us -> 117 us
    pallas_call x1, Pallas kernels: 138 us -> 117 us  [local(): pl.pallas_call(block_kernel, out_shape=jax.ShapeDtypeStruct((128, 2048),...]
where the time goes in v3:
time: 121 us
  Pallas kernels  117 us (97%)
  local copies, waits for them, and re-layouts  1.88 us (2%)
  between operations  1.31 us (1%)
    pallas_call x1, Pallas kernels, local(): pl.pallas_call(block_kernel, out_shape=jax.ShapeDtypeStruct((128, 2048),...  117 us

profile of v3, /device:TPU:24, one launch (start us, length us, event | category | flops | bytes accessed | tf_op | source)
XLA Modules:
  0.0 120.6 jit_solution(16432859851013734450)
XLA Ops:
  1.3 117.4 %block.1 = bf16[128,2048]{1,0:T(8,128)(2,1)} custom-call(s32[1]{0:T(128)S(6)} %copy.19.image_count, s32[1]{0:T(128)S(6)} %copy.20.prompt_count, bf16[2,4096]{1,0:T(2,128)(2,1)} %enc_own.1, bf16[128,3072]{1,0:T(8,128)(2,1)} %video.1, f32[2,3072]{1,0:T(2,128)} %bitcast.15, f32[2,3072]{1,0:T(2,128)} %bitcast.16, f32[1,4096]{1,0:T(1,128)} %bitcast.17, ...), custom_call_target="tpu_custom_call" | custom-call | tf_op jit(solution)/shard_map/block/pallas_call | solution.py:504
  118.7 1.9 %copy.21 = bf16[128,2048]{1,0:T(8,128)(2,1)} copy(bf16[128,2048]{1,0:T(8,128)(2,1)} %block.1) | data formatting | bytes 1048576
